TPU v7x, 32 devices: a whole 2x2x4 slice. The times are simulated.
32 devices in a mesh: dp: 16 (over z, x, core), tensor: 2 (over y).
Axes of the slice: x: 2, y: 2, z: 4, core: 2. Of those that a mesh axis runs over, the one named last changes fastest.
Arguments:
- hidden: bfloat16 [32, 1024, 1024], P('dp'), may hold values from -6 to 6
- segment_ids: int32 [32, 1024], P('dp'), may hold values from 0 to 3, never falling along the last dimension, each value on 1 to 800 neighbouring positions
- norm_gain: float32 [1024], replicated, may hold values from 0.1 to 1.9
- proj_gate: bfloat16 [1024, 2048], P(None, 'tensor'), may hold values from -0.1875 to 0.1875
- proj_value: bfloat16 [1024, 2048], P(None, 'tensor'), may hold values from -0.1875 to 0.1875
- proj_state: bfloat16 [1024, 256], replicated, may hold values from -0.1875 to 0.1875
- proj_step: bfloat16 [1024, 32], P(None, 'tensor'), may hold values from -0.1875 to 0.1875
- conv_value: float32 [4, 2048], P(None, 'tensor'), may hold values from -3 to 3
- conv_value_bias: float32 [2048], P('tensor'), may hold values from -3 to 3
- conv_state: float32 [4, 256], replicated, may hold values from -3 to 3
- conv_state_bias: float32 [256], replicated, may hold values from -3 to 3
- step_bias: float32 [32], P('tensor'), may hold values from -6 to -2
- decay_log: float32 [32], P('tensor'), may hold values from 0 to 2.77
- skip_gain: float32 [32], P('tensor'), may hold values from 0.5 to 1.5
- gate_gain: float32 [2048], P('tensor'), may hold values from 0.1 to 1.9
- proj_out: bfloat16 [1024, 2048], P(None, 'tensor'), may hold values from -0.125 to 0.125
- out_grad: bfloat16 [32, 1024, 1024], P('dp'), may hold values from -6 to 6
Outputs:
- block_out: bfloat16 [32, 1024, 1024], P('dp')
- grad_hidden: float32 [32, 1024, 1024], P('dp')
- grad_norm_gain: float32 [1024], replicated
- grad_proj_gate: float32 [1024, 2048], P('dp', 'tensor')
- grad_proj_value: float32 [1024, 2048], P('dp', 'tensor')
- grad_proj_state: float32 [1024, 256], P('dp')
- grad_proj_step: float32 [1024, 32], P('dp', 'tensor')
- grad_conv_value: float32 [4, 2048], P(None, 'tensor')
- grad_conv_value_bias: float32 [2048], P('tensor')
- grad_conv_state: float32 [4, 256], replicated
- grad_conv_state_bias: float32 [256], replicated
- grad_step_bias: float32 [32], P('tensor')
- grad_decay_log: float32 [32], P('tensor')
- grad_skip_gain: float32 [32], P('tensor')
- grad_gate_gain: float32 [2048], P('tensor')
- grad_proj_out: float32 [1024, 2048], P('dp', 'tensor')
Inputs may be any that keep to these rules, and one draw needn't show every extreme that they name: `segment_ids`: tokens of a sequence with the same number form one document; numbers never fall along a sequence; each sequence holds 4 documents of 1 to 800 tokens, one of exactly 800.
All inputs are finite; a program needn't handle non-finite values.
Results may differ from a plain program's by a relative error of at most 0.019.
Values sent between devices are 32-bit elements; how exact they have to be, the bound alone decides.
A program may use at most 192 MiB of HBM per device.

v0:
```python
import functools
import jax
import jax.numpy as jnp
from jax import lax
from jax.sharding import PartitionSpec as P

HEAD_DIM = 64
STATE = 128
KERNEL = 4
epsilon = 1e-05
precise = lax.Precision.HIGHEST


def lag_masks(segment_row):
    length = segment_row.shape[0]
    result = [jnp.ones((length,), jnp.float32)]
    for delay in range(1, KERNEL):
        earlier = jnp.concatenate(
            [jnp.full((delay,), -1, jnp.int32), segment_row[: length - delay]]
        )
        result.append((earlier == segment_row).astype(jnp.float32))
    return result


def causal_conv(values, weight, conv_bias, doc_masks):
    length = values.shape[0]
    summed = conv_bias[None, :] + weight[KERNEL - 1][None, :] * values
    for delay in range(1, KERNEL):
        earlier = jnp.concatenate(
            [jnp.zeros((delay, values.shape[1]), jnp.float32), values[: length - delay]], axis=0
        )
        summed = summed + weight[KERNEL - 1 - delay][None, :] * earlier * doc_masks[delay][:, None]
    return jax.nn.silu(summed)


CHUNK = 128


def head_mix(values, states, step_raw, segment_row, step_bias, decay_log, skip_gain):
    length, inner = values.shape
    heads = step_raw.shape[1]
    chunks = length // CHUNK
    step_size = jax.nn.softplus(step_raw + step_bias[None, :])
    decay_rate = -jnp.exp(decay_log)
    places = jnp.arange(CHUNK)
    lower = places[:, None] >= places[None, :]
    drop = (step_size * decay_rate[None, :]).reshape(chunks, CHUNK, heads)
    running = jnp.einsum("ts,csh->cth", lower.astype(jnp.float32), drop, precision=precise)
    segments = segment_row.reshape(chunks, CHUNK)
    last = segments[:, -1]
    before = jnp.concatenate([jnp.full((1,), -1, jnp.int32), last[:-1]])
    allowed = lower[None] & (segments[:, :, None] == segments[:, None, :])
    state_in = states[:, :STATE].astype(jnp.bfloat16).reshape(chunks, CHUNK, STATE)
    state_out = states[:, STATE:].astype(jnp.bfloat16).reshape(chunks, CHUNK, STATE)
    affinity = jnp.einsum("ctn,csn->cts", state_out, state_in, preferred_element_type=jnp.float32)
    running_head = running.transpose(0, 2, 1)
    step_head = step_size.reshape(chunks, CHUNK, heads).transpose(0, 2, 1)
    decays = jnp.exp(
        jnp.where(
            allowed[:, None], running_head[:, :, :, None] - running_head[:, :, None, :], -1e30
        )
    )
    mixing = (decays * affinity[:, None] * step_head[:, :, None, :]).astype(jnp.bfloat16)
    low_head = values.astype(jnp.bfloat16).reshape(chunks, CHUNK, heads, HEAD_DIM)
    near = jnp.einsum("chts,cshp->cthp", mixing, low_head, preferred_element_type=jnp.float32)
    near = near.reshape(chunks, CHUNK, inner)
    spread = (jnp.arange(inner)[None, :] // HEAD_DIM == jnp.arange(heads)[:, None]).astype(
        jnp.float32
    )
    total = running[:, -1, :]
    at_end = (segments == last[:, None]).astype(jnp.float32)
    from_start = (segments == before[:, None]).astype(jnp.float32)
    keep_scale = (
        jnp.exp(total[:, None, :] - running)
        * step_size.reshape(chunks, CHUNK, heads)
        * at_end[:, :, None]
    )
    read_scale = jnp.exp(running) * from_start[:, :, None]
    carry = jnp.exp(total) * (last == before).astype(jnp.float32)[:, None]
    keep_wide = jnp.einsum("cth,hi->cti", keep_scale, spread, precision=lax.Precision.HIGH)
    read_wide = jnp.einsum("cth,hi->cti", read_scale, spread, precision=lax.Precision.HIGH)
    carry_wide = jnp.einsum("ch,hi->ci", carry, spread, precision=precise)
    kept = (values.reshape(chunks, CHUNK, inner) * keep_wide).astype(jnp.bfloat16)
    gained = jnp.einsum("csn,csi->cni", state_in, kept, preferred_element_type=jnp.float32)
    held = jnp.zeros((STATE, inner), jnp.float32)
    entry = []
    for c in range(chunks):
        entry.append(held.astype(jnp.bfloat16))
        held = held * carry_wide[c][None, :] + gained[c]
    entry = jnp.stack(entry)
    far = jnp.einsum("ctn,cni->cti", state_out, entry, preferred_element_type=jnp.float32)
    mixed = (near + far * read_wide).reshape(length, inner)
    return mixed + jnp.repeat(skip_gain, HEAD_DIM)[None, :] * values


def mixer(
    segment_row,
    value_row,
    state_row,
    step_row,
    conv_value,
    conv_value_bias,
    conv_state,
    conv_state_bias,
    step_bias,
    decay_log,
    skip_gain,
):
    doc_masks = lag_masks(segment_row)
    value_conv = causal_conv(value_row, conv_value, conv_value_bias, doc_masks)
    state_conv = causal_conv(state_row, conv_state, conv_state_bias, doc_masks)
    return head_mix(value_conv, state_conv, step_row, segment_row, step_bias, decay_log, skip_gain)


def right_product(left, weight):
    return lax.dot_general(
        left, weight, (((1,), (1,)), ((), ())), preferred_element_type=jnp.float32
    )


def token_product(left, right):
    return lax.dot_general(
        left, right, (((0,), (0,)), ((), ())), preferred_element_type=jnp.float32
    )


def tensor_others(part):
    count = lax.axis_size("tensor")
    if count == 2:
        return lax.ppermute(part, "tensor", [(0, 1), (1, 0)])
    return lax.psum(part, "tensor")


def tensor_join(part, others):
    return part + others if lax.axis_size("tensor") == 2 else others


def after(value, *earlier):
    return lax.optimization_barrier((value, *earlier))[0]


def local(
    hidden,
    segment_ids,
    norm_gain,
    proj_gate,
    proj_value,
    proj_state,
    proj_step,
    conv_value,
    conv_value_bias,
    conv_state,
    conv_state_bias,
    step_bias,
    decay_log,
    skip_gain,
    gate_gain,
    proj_out,
    out_grad,
):
    seq_count, length, width = hidden.shape
    local_inner = proj_gate.shape[1]
    local_heads = proj_step.shape[1]
    state_width = proj_state.shape[1]
    tensor_count = lax.axis_size("tensor")
    inner_total = local_inner * tensor_count
    every = range(seq_count)
    wides = [hidden[s].astype(jnp.float32) for s in every]
    row_scales = [lax.rsqrt(jnp.mean(w * w, axis=-1, keepdims=True) + epsilon) for w in wides]
    normeds = [(w * r * norm_gain[None, :]).astype(jnp.bfloat16) for w, r in zip(wides, row_scales)]
    params = (
        conv_value,
        conv_value_bias,
        conv_state,
        conv_state_bias,
        step_bias,
        decay_log,
        skip_gain,
    )
    gate_raws, mixed_outs, mixer_backs, gateds, squares = ([], [], [], [], [])
    for s in every:
        gate_raw = jnp.dot(normeds[s], proj_gate, preferred_element_type=jnp.float32)
        value_raw = jnp.dot(normeds[s], proj_value, preferred_element_type=jnp.float32)
        state_raw = jnp.dot(normeds[s], proj_state, preferred_element_type=jnp.float32)
        step_raw = jnp.dot(normeds[s], proj_step, preferred_element_type=jnp.float32)
        mixed_out, back = jax.vjp(
            jax.checkpoint(functools.partial(mixer, segment_ids[s])),
            value_raw,
            state_raw,
            step_raw,
            *params
        )
        gated = mixed_out * jax.nn.silu(gate_raw)
        gate_raws.append(gate_raw)
        mixed_outs.append(mixed_out)
        mixer_backs.append(back)
        gateds.append(gated)
        squares.append(jnp.sum(gated * gated, axis=-1))
    d_output_ins = [
        jnp.dot(out_grad[s], proj_out, preferred_element_type=jnp.float32) for s in every
    ]
    inners = [jnp.sum(d_output_ins[s] * gate_gain[None, :] * gateds[s], axis=-1) for s in every]
    both = lax.psum(jnp.stack(squares + inners), "tensor")
    branches, received, output_ins, d_gates, d_mixeds = ([], [], [], [], [])
    grad_gate_gain = jnp.zeros((local_inner,), jnp.float32)
    for s in every:
        gated, gate_raw = (gateds[s], gate_raws[s])
        gated_scale = lax.rsqrt(both[s] / inner_total + epsilon)[:, None]
        gate_inner = both[seq_count + s][:, None]
        output_in = (gated * gated_scale * gate_gain[None, :]).astype(jnp.bfloat16)
        branches.append(right_product(output_in, proj_out))
        received.append(tensor_others(branches[s]))
        d_output_in = d_output_ins[s]
        grad_gate_gain = grad_gate_gain + jnp.sum(d_output_in * gated * gated_scale, axis=0)
        weighted = d_output_in * gate_gain[None, :]
        d_gated = gated_scale * weighted - gated_scale**3 * gated * gate_inner / inner_total
        sigma = jax.nn.sigmoid(gate_raw)
        d_mixeds.append(d_gated * gate_raw * sigma)
        d_gates.append(
            (d_gated * mixed_outs[s] * sigma * (1.0 + gate_raw * (1.0 - sigma))).astype(
                jnp.bfloat16
            )
        )
        output_ins.append(output_in)
    normed_all = jnp.concatenate(normeds, axis=0)
    early_part = jnp.concatenate(
        [
            token_product(normed_all, jnp.concatenate(d_gates, axis=0)),
            token_product(
                out_grad.reshape(seq_count * length, width), jnp.concatenate(output_ins, axis=0)
            ),
        ],
        axis=1,
    )
    early = lax.psum_scatter(early_part, "dp", scatter_dimension=0, tiled=True)
    late_weight = jnp.concatenate([proj_value, proj_state, proj_step], axis=1)
    param_grads, lates, parts, others, grad_hiddens = (None, [], [], [], [])
    waits = (early_part, *branches)
    grad_norm_gain = jnp.zeros((width,), jnp.float32)
    for s in every:
        d_value, d_state, d_step, *grads = mixer_backs[s](after(d_mixeds[s], *waits))
        param_grads = grads if s == 0 else [a + b for a, b in zip(param_grads, grads)]
        late = jnp.concatenate([d_value, d_state, d_step], axis=1).astype(jnp.bfloat16)
        lates.append(late)
        part = right_product(d_gates[s], proj_gate) + right_product(late, late_weight)
        grad_norm_gain = grad_norm_gain + jnp.sum(part * wides[s] * row_scales[s], axis=0)
        parts.append(part)
        if s < seq_count - 1:
            parts[s] = after(part, received[s])
            others.append(tensor_others(parts[s]))
            waits = (part, received[s])
    edge_state = local_inner + state_width
    g_cv, g_cvb, g_cs, g_csb, g_sb, g_dl, g_sg = param_grads
    own = [g_cv, g_cvb, g_sb, g_dl, g_sg, grad_gate_gain]
    shared = [g_cs, g_csb, grad_norm_gain]
    own_flat = jnp.concatenate([g.reshape(-1) for g in own])
    place = lax.axis_index("tensor")
    mine = (jnp.arange(tensor_count) == place)[:, None]
    slots = jnp.where(mine, own_flat[None, :], 0.0).reshape(-1)
    packed = lax.psum(
        after(
            jnp.concatenate([slots] + [g.reshape(-1) for g in shared]), early, received[-1], *others
        ),
        ("dp", "tensor"),
    )
    own_sum = lax.dynamic_slice(packed, (place * own_flat.shape[0],), (own_flat.shape[0],))
    shared_sum = packed[slots.shape[0] :]
    later = lax.psum_scatter(
        token_product(normed_all, after(jnp.concatenate(lates, axis=0), packed)),
        "dp",
        scatter_dimension=0,
        tiled=True,
    )
    block_outs = []
    for s in every:
        if s == seq_count - 1:
            parts[s] = after(parts[s], packed)
            others.append(tensor_others(parts[s]))
        d_scaled = tensor_join(parts[s], others[s]) * norm_gain[None, :]
        row_scale, wide = (row_scales[s], wides[s])
        norm_inner = jnp.sum(d_scaled * wide, axis=-1, keepdims=True)
        grad_hiddens.append(
            out_grad[s].astype(jnp.float32)
            + row_scale * d_scaled
            - row_scale**3 * wide * norm_inner / width
        )
        branch = tensor_join(branches[s], received[s])
        block_outs.append((wide + branch).astype(jnp.bfloat16))
    grad_proj_state = lax.psum(later[:, local_inner:edge_state], "tensor")

    def split(flat, like):
        result, edge = ([], 0)
        for g in like:
            result.append(flat[edge : edge + g.size].reshape(g.shape))
            edge += g.size
        return result

    r_cv, r_cvb, r_sb, r_dl, r_sg, r_gg = split(own_sum, own)
    r_cs, r_csb, r_ng = split(shared_sum, shared)
    return (
        jnp.stack(block_outs),
        jnp.stack(grad_hiddens),
        r_ng,
        early[:, :local_inner],
        later[:, :local_inner],
        grad_proj_state,
        later[:, edge_state:],
        r_cv,
        r_cvb,
        r_cs,
        r_csb,
        r_sb,
        r_dl,
        r_sg,
        r_gg,
        early[:, local_inner:],
    )


def solution(mesh):
    in_specs = (
        P("dp", None, None),
        P("dp", None),
        P(),
        P(None, "tensor"),
        P(None, "tensor"),
        P(),
        P(None, "tensor"),
        P(None, "tensor"),
        P("tensor"),
        P(),
        P(),
        P("tensor"),
        P("tensor"),
        P("tensor"),
        P("tensor"),
        P(None, "tensor"),
        P("dp", None, None),
    )
    out_specs = (
        P("dp", None, None),
        P("dp", None, None),
        P(),
        P("dp", "tensor"),
        P("dp", "tensor"),
        P("dp", None),
        P("dp", "tensor"),
        P(None, "tensor"),
        P("tensor"),
        P(),
        P(),
        P("tensor"),
        P("tensor"),
        P("tensor"),
        P("tensor"),
        P("dp", "tensor"),
    )
    return jax.shard_map(local, mesh=mesh, in_specs=in_specs, out_specs=out_specs, check_vma=False)
```

profile of v0, /device:TPU:0, one launch (start us, length us, event | category | flops | bytes accessed | tf_op | source)
XLA Modules:
  0.0 794.7 jit_solution(9242613608619532424)
XLA Ops:
  50.2 22.6 %fusion.435 = (bf16[1024,1024]{1,0:T(8,128)(2,1)}, f32[1024,1024]{1,0:T(8,128)}, bf16[1024,1024]{1,0:T(8,128)(2,1)}, f32[1024,1024]{1,0:T(8,128)S(1)}) fusion(f32[1024]{0:T(1024)S(1)} %get-tuple-element.468, f32[1021,1024]{1,0:T(8,128)} %bitcast.722, f32[1024]{0:T(1024)S(1)} %bitcast.950, f32[1024]{0:T(1024)S(1)} %get-tuple-element.467, ...), kind=kLoop, calls=%fused_computation.717 | loop fusion | flops 33554432 | bytes 46133248 | tf_op jit(solution)/shard_map/jvp()/convert_element_type | solution.py:64
  116.5 7.6 fusion.18
  144.4 14.7 %multiply_reduce_fusion.15 = (f32[1024]{0:T(1024)S(1)}, f32[1024]{0:T(1024)S(1)}, f32[1024,1024]{1,0:T(8,128)}, f32[1024]{0:T(1024)S(1)}, f32[1024]{0:T(1024)S(1...) fusion(f32[1024]{0:T(1024)S(1)} %copy-done.208, f32[1024,1024]{1,0:T(8,128)} %fusion.465, ...), kind=kOutput, calls=%fused_computation.169 | convolution fusion | flops 2172645376 | bytes 46161920 | tf_op jit(solution)/shard_map/dot_general | solution.py:200
  159.1 9.7 %psum.21 = f32[4,1024]{1,0:T(4,128)S(1)} all-reduce(f32[4,1024]{1,0:T(4,128)S(1)} %pad_maximum_fusion.9), channel_id=1, replica_groups=mesh['dp'=16,'tensor'=2] {'tensor'}, use_global_device_ids=true, to_apply=%region_6.7 | all-reduce | flops 4096 | bytes 32768 | tf_op jit(solution)/shard_map/psum | solution.py:203
  168.9 19.2 %multiply_multiply_fusion.1 = (f32[1024,1024]{1,0:T(8,128)}, bf16[1024,1024]{1,0:T(8,128)(2,1)S(1)}, f32[1024]{0:T(1024)}, bf16[1024,1024]{1,0:T(8,128)(2,1)S(1)...) fusion(f32[1024,1024]{1,0:T(8,128)} %fusion.465, ...), kind=kLoop, calls=%fused_computation.152 | loop fusion | flops 54523904 | bytes 58761216 | tf_op jit(solution)/shard_map/mul | solution.py:218
  208.3 9.2 %copy.351 = f32[1024,2048]{1,0:T(8,128)} copy(f32[1024,2048]{0,1:T(8,128)} %pad_maximum_fusion) | data formatting | bytes 16777216
  248.1 13.2 %multiply_reduce_fusion.3 = (f32[1024]{0:T(1024)}, f32[1024,1024]{1,0:T(8,128)S(1)}, f32[1024,1024]{1,0:T(8,128)}) fusion(f32[1024,1024]{1,0:T(8,128)} %get-tuple-element.53, f32[1024]{0:T(1024)} %copy-done.130, f32[1021,1024]{1,0:T(8,128)} %bitcast.725, f32[1024]{0:T(1024)} %bitcast.927, f32[1024]{0:T(1024)} %copy-done.125, f32[1022,1024]{1,0:T(8,128)} %bitcast.726, ...), kind=kLoop, calls=%fused_computation.115 | loop fusion | flops 17824768 | bytes 29372416 | tf_op jit(solution)/shard_map/transpose(jvp(jvp()))/checkpoint/reduce_sum | solution.py:93
  294.8 7.7 reshape.1878
  305.1 11.4 %multiply_reduce_fusion.11 = (f32[1024]{0:T(1024)}, f32[1024,1024]{1,0:T(8,128)S(1)}, f32[1024,1024]{1,0:T(8,128)}) fusion(f32[1021,1024]{1,0:T(8,128)} %bitcast.728, f32[1024]{0:T(1024)} %copy-done.130, f32[1024,1024]{1,0:T(8,128)} %get-tuple-element.223, f32[1024,1024]{1,0:T(8,128)} %reshape.1878, f32[8,128,1024]{2,1,0:T(8,128)} %get-tuple-element.312, ...), kind=kLoop, calls=%fused_computation.123 | loop fusion | flops 15727616 | bytes 29360128 | tf_op jit(solution)/shard_map/transpose(jvp(jvp()))/checkpoint/reduce_sum | solution.py:32
  325.8 12.3 %fusion.15 = (f32[8,16,128]{2,1,0:T(8,128)}, f32[8,16,128]{2,1,0:T(8,128)}, f32[8,16,128]{2,1,0:T(8,128)S(1)}, bf16[8,128,128]{2,1,0:T(8,128)(2,1)S(1)}) fusion(f32[8,16,128]{2,1,0:T(8,128)} %copy.296, f32[8,128,128]{2,1,0:T(8,128)} %fusion.476, f32[8,16,128]{2,1,0:T(8,128)S(1)} %fusion.291, pred[8,128,128]{2,1,0:T(8,128)(4,1)} %compare_and_fusion.1, ...), kind=kOutput, calls=%fused_computation.39 | convolution fusion | flops 297615360 | bytes 5439488 | tf_op jit(solution)/shard_map/transpose(jvp(jvp()))/checkpoint/chts,cshp->cthp/dot_general | solution.py:65
  385.5 8.5 %fusion.135 = f32[1024,1024]{1,0:T(8,128)} fusion(f32[1024,1024]{1,0:T(8,128)} %fusion.475, bf16[1024,16]{1,0:T(8,128)(2,1)S(1)} %get-tuple-element.227, bf16[1024,256]{1,0:T(8,128)(2,1)S(1)} %get-tuple-element.318, bf16[1024,1024]{1,0:T(8,128)(2,1)S(1)} %get-tuple-element.304, bf16[1024,16]{1,0:T(8,128)(2,1)S(1)} %copy-done.96, ...), kind=kOutput, calls=%fused_computation.223 | convolution fusion | flops 2734882816 | bytes 13697024 | tf_op jit(solution)/shard_map/dot_general | solution.py:116
  421.2 7.6 reshape.1880
  438.3 13.2 %multiply_reduce_fusion.2 = (f32[1024]{0:T(1024)}, f32[1024,1024]{1,0:T(8,128)S(1)}, f32[1024,1024]{1,0:T(8,128)}) fusion(f32[1024,1024]{1,0:T(8,128)} %get-tuple-element.69, f32[1024]{0:T(1024)} %copy-done.128, f32[1021,1024]{1,0:T(8,128)} %bitcast.716, f32[1024]{0:T(1024)} %bitcast.925, f32[1024]{0:T(1024)} %copy-done.120, f32[1022,1024]{1,0:T(8,128)} %bitcast.717, ...), kind=kLoop, calls=%fused_computation.114 | loop fusion | flops 17824768 | bytes 29372416 | tf_op jit(solution)/shard_map/transpose(jvp(jvp()))/checkpoint/reduce_sum | solution.py:93
  461.6 11.3 %fusion.17 = (f32[8,16,128]{2,1,0:T(8,128)}, f32[8,16,128]{2,1,0:T(8,128)}, f32[8,16,128]{2,1,0:T(8,128)S(1)}, bf16[8,128,128]{2,1,0:T(8,128)(2,1)}) fusion(f32[8,16,128]{2,1,0:T(8,128)S(1)} %copy-done.141, f32[8,128,128]{2,1,0:T(8,128)S(1)} %fusion.480, f32[8,16,128]{2,1,0:T(8,128)S(1)} %fusion.288, pred[8,128,128]{2,1,0:T(8,128)(4,1)S(1)} %copy-done.105, ...), kind=kOutput, calls=%fused_computation.41 | convolution fusion | flops 297615360 | bytes 5439488 | tf_op jit(solution)/shard_map/transpose(jvp(jvp()))/checkpoint/chts,cshp->cthp/dot_general | solution.py:65
  500.0 9.2 %multiply_reduce_fusion.7 = (f32[1024]{0:T(1024)S(1)}, f32[1024,1024]{1,0:T(8,128)S(1)}, f32[1024,1024]{1,0:T(8,128)S(1)}) fusion(f32[1021,1024]{1,0:T(8,128)} %bitcast.719, f32[1024]{0:T(1024)S(1)} %copy-done.129, f32[1024,1024]{1,0:T(8,128)} %get-tuple-element.220, f32[1024,1024]{1,0:T(8,128)} %reshape.1880, f32[8,128,1024]{2,1,0:T(8,128)} %get-tuple-element.308, ...), kind=kLoop, calls=%fused_computation.119 | loop fusion | flops 15727616 | bytes 29360128 | tf_op jit(solution)/shard_map/transpose(jvp(jvp()))/checkpoint/reduce_sum | solution.py:32
  526.3 9.6 %fusion.44 = (f32[1024]{0:T(1024)S(1)}, f32[1024]{0:T(1024)S(1)}, f32[1024,1024]{1,0:T(8,128)}) fusion(f32[1024]{0:T(1024)S(1)} %copy-done.152, bf16[2,1024,1024]{2,1,0:T(8,128)(2,1)} %param.18, f32[1024]{0:T(1024)S(1)} %copy-done.154, f32[1024,1024]{1,0:T(8,128)} %fusion.135, f32[1024,1024]{1,0:T(8,128)} %fusion.479, bf16[1024,16]{1,0:T(8,128)(2,1)} %copy.309, ...), kind=kOutput, calls=%fused_computation.75 | convolution fusion | flops 2743269376 | bytes 22102016 | tf_op jit(solution)/shard_map/dot_general | solution.py:116
  536.0 26.3 %maximum_maximum_fusion = bf16[2048,1296]{1,0:T(8,128)(2,1)} fusion(bf16[1024,16]{1,0:T(8,128)(2,1)} %get-tuple-element.225, bf16[1024,256]{1,0:T(8,128)(2,1)S(1)} %get-tuple-element.319, bf16[1024,1024]{1,0:T(8,128)(2,1)} %get-tuple-element.305, bf16[1024,16]{1,0:T(8,128)(2,1)S(1)} %get-tuple-element.227, bf16[1024,256]{1,0:T(8,128)(2,1)S(1)} %copy-done.63, ...), kind=kLoop, calls=%fused_computation.44 | loop fusion | flops 31850496 | bytes 10616832 | tf_op jit(solution)/shard_map/concatenate | solution.py:269
  563.7 25.9 %collective-permute-done.2 = f32[1024,1024]{1,0:T(8,128)} collective-permute-done((f32[1024,1024]{1,0:T(8,128)}, f32[1024,1024]{1,0:T(8,128)}, u32[]{:S(2)}, u32[]{:S(2)}) %collective-permute-start.2) | collective-permute-done | bytes 4194336 | tf_op jit(solution)/shard_map/ppermute | solution.py:130
  589.6 40.5 %psum.22 = f32[14688]{0:T(1024)S(1)} all-reduce(f32[14688]{0:T(1024)S(1)} %concatenate.230), channel_id=1, replica_groups=mesh['dp'=16,'tensor'=2] {'dp','tensor'}, use_global_device_ids=true, to_apply=%region_65.67 | all-reduce | flops 14688 | bytes 117504 | tf_op jit(solution)/shard_map/psum | solution.py:260
  630.2 11.5 %fusion.112 = f32[1024,1296]{1,0:T(8,128)} fusion(bf16[2048,1296]{1,0:T(8,128)(2,1)} %maximum_maximum_fusion, bf16[1024,1024]{1,0:T(8,128)(2,1)} %copy-done.43, bf16[1024,1024]{1,0:T(8,128)(2,1)S(1)} %copy-done.42), kind=kOutput, calls=%fused_computation.204 | convolution fusion | flops 5444206592 | bytes 14811136 | tf_op jit(solution)/shard_map/dot_general | solution.py:122
  649.3 84.6 %collective-permute-done.3 = f32[1024,1024]{1,0:T(8,128)} collective-permute-done((f32[1024,1024]{1,0:T(8,128)}, f32[1024,1024]{1,0:T(8,128)}, u32[]{:S(2)}, u32[]{:S(2)}) %collective-permute-start.3) | collective-permute-done | bytes 4194336 | tf_op jit(solution)/shard_map/ppermute | solution.py:130
  734.0 11.7 %fusion.36 = (f32[1024]{0:T(1024)S(1)}, f32[1024]{0:T(1024)S(1)}, bf16[1,1024,1024]{2,1,0:T(8,128)(2,1)}) fusion(f32[1024]{0:T(1024)S(1)} %copy-done.148, f32[1024,1024]{1,0:T(8,128)} %fusion.135, f32[1024,1024]{1,0:T(8,128)} %collective-permute-done.2, bf16[2,1024,1024]{2,1,0:T(8,128)(2,1)} %param.18, f32[1024,1024]{1,0:T(8,128)} %get-tuple-element.82, ...), kind=kLoop, calls=%fused_computation.67 | loop fusion | flops 13629440 | bytes 31469568 | tf_op jit(solution)/shard_map/reduce_sum | solution.py:281
  745.8 11.8 %fusion.35 = (f32[1,1024,1024]{2,1,0:T(8,128)S(1)}, f32[1,1024,1024]{2,1,0:T(8,128)}, bf16[1,1024,1024]{2,1,0:T(8,128)(2,1)}) fusion(f32[1024]{0:T(1024)S(1)} %get-tuple-element.178, f32[1024]{0:T(1024)S(1)} %copy-done.176, f32[1024]{0:T(1024)S(1)} %copy-done.154, bf16[2,1024,1024]{2,1,0:T(8,128)(2,1)} %param.34, f32[1024]{0:T(1024)S(1)} %copy-done.148, ...), kind=kLoop, calls=%fused_computation.66 | loop fusion | flops 24117248 | bytes 44068864 | tf_op jit(solution)/shard_map/stack | solution.py:302
  772.1 14.4 %all-reduce.96.cloned.1.call-done = f32[64,256]{1,0:T(8,128)} async-done(((f32[64,256]{1,0:T(8,128)}), f32[64,256]{1,0:T(8,128)}) %all-reduce.96.cloned.1.call-update) | async-done | bytes 65552 | tf_op jit(solution)/shard_map/psum | solution.py:289
  (766 shorter events, 364.0 us)
Async XLA Ops:
  7.2 122.4 %copy-start = (bf16[1024,1024]{1,0:T(8,128)(2,1)S(1)}, bf16[1024,1024]{1,0:T(8,128)(2,1)}, u32[]{:S(2)}) copy-start(bf16[1024,1024]{1,0:T(8,128)(2,1)} %param.33) | copy-start | bytes 6291460
  7.2 555.1 %reduce-scatter.7.cloned.1.call-start = ((), (), s32[]{:S(2)}) async-start(), calls=%async_computation.4 | async-start | bytes 8912896
  8.1 77.9 %copy-start.72 = (s32[1,1024]{1,0:T(1,128)}, s32[1,1024]{1,0:T(1,128)S(1)}, u32[]{:S(2)}) copy-start(s32[1,1024]{1,0:T(1,128)S(1)} %get-tuple-element.415) | copy-start | bytes 12292
  16.0 14.7 %copy-start.40 = (bf16[1024,1024]{1,0:T(8,128)(2,1)}, bf16[1024,1024]{1,0:T(8,128)(2,1)S(1)}, u32[]{:S(2)}) copy-start(bf16[1024,1024]{1,0:T(8,128)(2,1)S(1)} %get-tuple-element.300) | copy-start | bytes 6291460
  16.0 19.0 %copy-start.43 = (bf16[1024,1024]{1,0:T(8,128)(2,1)}, bf16[1024,1024]{1,0:T(8,128)(2,1)S(1)}, u32[]{:S(2)}) copy-start(bf16[1024,1024]{1,0:T(8,128)(2,1)S(1)} %get-tuple-element.301) | copy-start | bytes 6291460
  26.3 13.8 %copy-start.75 = (f32[1024,16]{0,1:T(8,128)}, f32[1024,16]{0,1:T(8,128)S(1)}, u32[]{:S(2)}) copy-start(f32[1024,16]{0,1:T(8,128)S(1)} %fusion.467) | copy-start | bytes 196612
  28.9 12.8 %copy-start.5 = (f32[1024,256]{1,0:T(8,128)}, f32[1024,256]{1,0:T(8,128)S(1)}, u32[]{:S(2)}) copy-start(f32[1024,256]{1,0:T(8,128)S(1)} %fusion.468) | copy-start | bytes 3145732
  29.9 195.1 %copy-start.94 = (pred[128,128]{1,0:T(8,128)(4,1)}, pred[128,128]{1,0:T(8,128)(4,1)S(1)}, u32[]{:S(2)}) copy-start(pred[128,128]{1,0:T(8,128)(4,1)S(1)} %iota_compare_fusion.7) | copy-start | bytes 49156
  50.2 22.6 %copy-start.179 = (f32[8,16]{1,0:T(8,128)S(1)}, f32[8,16]{1,0:T(8,128)}, u32[]{:S(2)}) copy-start(f32[8,16]{1,0:T(8,128)} %copy-done.178) | copy-start | bytes 1540
  192.6 201.4 %collective-permute-start = (f32[1024,1024]{1,0:T(8,128)}, f32[1024,1024]{1,0:T(8,128)}, u32[]{:S(2)}, u32[]{:S(2)}) collective-permute-start(f32[1024,1024]{1,0:T(8,128)} %fusion.473), channel_id=1, source_target_pairs={{0,1},{1,0},{2,3},{3,2},{4,5},{5,4},{6,7},{7,6},{8,9},{9,8},{10,11... | collective-permute-start | bytes 12582920 | tf_op jit(solution)/shard_map/ppermute | solution.py:130
  217.6 546.8 %reduce-scatter.5.cloned.1.call-start = ((), (), s32[]{:S(2)}) async-start(), calls=%async_computation.2 | async-start | bytes 6127616 | tf_op jit(solution)/shard_map/reduce_scatter | solution.py:268
  223.7 340.0 %collective-permute-start.1 = (f32[1024,1024]{1,0:T(8,128)}, f32[1024,1024]{1,0:T(8,128)}, u32[]{:S(2)}, u32[]{:S(2)}) collective-permute-start(f32[1024,1024]{1,0:T(8,128)} %fusion.474), channel_id=1, source_target_pairs={{0,1},{1,0},{2,3},{3,2},{4,5},{5,4},{6,7},{7,6},{8,9},{9,8},{10,11... | collective-permute-start | bytes 12582920 | tf_op jit(solution)/shard_map/ppermute | solution.py:130
  363.7 21.7 %copy-start.62 = (bf16[1024,256]{1,0:T(8,128)(2,1)}, bf16[1024,256]{1,0:T(8,128)(2,1)S(1)}, u32[]{:S(2)}) copy-start(bf16[1024,256]{1,0:T(8,128)(2,1)S(1)} %get-tuple-element.318) | copy-start | bytes 1572868
  499.2 90.4 %collective-permute-start.2 = (f32[1024,1024]{1,0:T(8,128)}, f32[1024,1024]{1,0:T(8,128)}, u32[]{:S(2)}, u32[]{:S(2)}) collective-permute-start(f32[1024,1024]{1,0:T(8,128)} %fusion.135), channel_id=1, source_target_pairs={{0,1},{1,0},{2,3},{3,2},{4,5},{5,4},{6,7},{7,6},{8,9},{9,8},{10,11... | collective-permute-start | bytes 12582920 | tf_op jit(solution)/shard_map/ppermute | solution.py:130
  536.0 94.1 %copy-start.42 = (bf16[1024,1024]{1,0:T(8,128)(2,1)S(1)}, bf16[1024,1024]{1,0:T(8,128)(2,1)}, u32[]{:S(2)}) copy-start(bf16[1024,1024]{1,0:T(8,128)(2,1)} %copy-done.40) | copy-start | bytes 6291460
  641.7 92.3 %copy-start.148 = (f32[1024]{0:T(1024)S(1)}, f32[1024]{0:T(1024)}, u32[]{:S(2)}) copy-start(f32[1024]{0:T(1024)} %param.20) | copy-start | bytes 12292
  641.7 144.8 %all-reduce.96.cloned.1.call-start = ((), (), s32[]{:S(2)}) async-start(), calls=%async_computation.3 | async-start | bytes 131072 | tf_op jit(solution)/shard_map/psum | solution.py:289
  642.0 92.0 %collective-permute-start.3 = (f32[1024,1024]{1,0:T(8,128)}, f32[1024,1024]{1,0:T(8,128)}, u32[]{:S(2)}, u32[]{:S(2)}) collective-permute-start(f32[1024,1024]{1,0:T(8,128)} %get-tuple-element.82), channel_id=1, source_target_pairs={{0,1},{1,0},{2,3},{3,2},{4,5},{5,4},{6,7},{7,6},{8,9},{9,8},{10,11... | collective-permute-start | bytes 12582920 | tf_op jit(solution)/shard_map/ppermute | solution.py:130
  649.3 96.4 %copy-start.9 = (bf16[2,1024,1024]{2,1,0:T(8,128)(2,1)S(1)}, bf16[2,1024,1024]{2,1,0:T(8,128)(2,1)}, u32[]{:S(2)}) copy-start(bf16[2,1024,1024]{2,1,0:T(8,128)(2,1)} %param.18) | copy-start | bytes 12582916
  649.3 96.4 %copy-start.25 = (f32[1024,1024]{1,0:T(8,128)S(1)}, f32[1024,1024]{1,0:T(8,128)}, u32[]{:S(2)}) copy-start(f32[1024,1024]{1,0:T(8,128)} %fusion.135) | copy-start | bytes 12582916
  649.3 96.4 %copy-start.26 = (f32[1024,1024]{1,0:T(8,128)S(1)}, f32[1024,1024]{1,0:T(8,128)}, u32[]{:S(2)}) copy-start(f32[1024,1024]{1,0:T(8,128)} %get-tuple-element.82) | copy-start | bytes 12582916
  649.3 96.4 %copy-start.175 = (f32[1024]{0:T(1024)S(1)}, f32[1024]{0:T(1024)}, u32[]{:S(2)}) copy-start(f32[1024]{0:T(1024)} %get-tuple-element.420) | copy-start | bytes 12292
  649.3 96.4 %copy-start.176 = (f32[1024]{0:T(1024)S(1)}, f32[1024]{0:T(1024)}, u32[]{:S(2)}) copy-start(f32[1024]{0:T(1024)} %get-tuple-element.466) | copy-start | bytes 12292
  765.9 22.1 %copy-start.1 = (bf16[1024,1024]{1,0:T(8,128)(2,1)S(1)}, bf16[1024,1024]{1,0:T(8,128)(2,1)}, u32[]{:S(2)}) copy-start(bf16[1024,1024]{1,0:T(8,128)(2,1)} %param.33) | copy-start | bytes 6291460
  (221 other events, 936.8 us)
Sparse Core Ops, SparseCore 0:
  217.7 105.6 reduce-scatter.6
  641.8 81.9 reduce-scatter.4
  766.0 20.4 all-reduce.95
where the time goes:
time: 806 us; the launch traced here: 795 us
  other arithmetic  237 us (29%)
  matrix products  220 us (27%)
  local copies, waits for them, and re-layouts  142 us (18%)
  waiting for transfers between devices  125 us (16%)
  blocking collectives  50.2 us (6%)
  between operations  16.9 us (2%)
    ppermute x4, waiting for transfers between devices, tensor_others(): return lax.ppermute(part, 'tensor', [(0, 1), (1, 0)])  111 us
    dot_general x6, matrix products, head_mix(): jnp.einsum('chts,cshp->cthp', mixing, low_head, preferred_element_type=jn...  50.7 us
    psum x1, blocking collectives, local(): lax.psum(after(jnp.concatenate([slots] + [g.reshape(-1) for g in shared])...  40.5 us
    unnamed x495, local copies, waits for them, and re-layouts  39.8 us
    dot_general x6, matrix products, right_product(): lax.dot_general(left, weight, (((1,), (1,)), ((), ())), preferred_element...  37.4 us
    reduce_sum x8, other arithmetic, causal_conv(): weight[KERNEL - 1 - delay][None, :] * earlier * doc_masks[delay][:, None]  30.8 us
    convert_element_type x4, local copies, waits for them, and re-layouts, head_mix(): values.astype(jnp.bfloat16).reshape(chunks, CHUNK, heads, HEAD_DIM)  29.8 us
    reduce_sum x4, other arithmetic, head_mix(): return mixed + jnp.repeat(skip_gain, HEAD_DIM)[None, :] * values  27.3 us
  transfers between devices with their start and end apart: 7, of which 3 were waited for; matrix products, arithmetic and copies ran while one was open for 50% of the time, Pallas kernels for 0%

commit v1 on v0

--- a/solution.py
+++ b/solution.py
@@ -257,11 +257,17 @@
     place = lax.axis_index("tensor")
     mine = (jnp.arange(tensor_count) == place)[:, None]
     slots = jnp.where(mine, own_flat[None, :], 0.0).reshape(-1)
-    packed = lax.psum(
-        after(
-            jnp.concatenate([slots] + [g.reshape(-1) for g in shared]), early, received[-1], *others
+    packed = jnp.sum(
+        lax.all_gather(
+            after(
+                jnp.concatenate([slots] + [g.reshape(-1) for g in shared]),
+                early,
+                received[-1],
+                *others
+            ),
+            ("dp", "tensor"),
         ),
-        ("dp", "tensor"),
+        axis=0,
     )
     own_sum = lax.dynamic_slice(packed, (place * own_flat.shape[0],), (own_flat.shape[0],))
     shared_sum = packed[slots.shape[0] :]

time: 806 us -> 903 us (1.12)
  waiting for transfers between devices: 125 us -> 243 us
  blocking collectives: 50.2 us -> 9.67 us
  local copies, waits for them, and re-layouts: 142 us -> 159 us
    unnamed x4 -> x6, waiting for transfers between devices: 0.05 us -> 119 us
    psum x1 -> x0, blocking collectives: 40.5 us -> none  [local(): lax.psum(after(jnp.concatenate([slots] + [g.reshape(-1) for g in shared])...]
    concatenate x1, other arithmetic: 26.3 us -> 14 us  [local(): jnp.concatenate(lates, axis=0)]
    reshape x2, local copies, waits for them, and re-layouts: 10.9 us -> 21.6 us  [head_mix(): near = near.reshape(chunks, CHUNK, inner)]
    mul x12, other arithmetic: 11.4 us -> 20.8 us  [causal_conv(): weight[KERNEL - 1 - delay][None, :] * earlier * doc_masks[delay][:, None]]
    unnamed x495 -> x499, local copies, waits for them, and re-layouts: 39.8 us -> 44.9 us
  transfers between devices with their start and end apart: 7 -> 8, of which waited for: 3 -> 4; matrix products, arithmetic and copies ran while one was open for 50% -> 44% of each run, Pallas kernels for 0% -> 0%
where the time goes in v1:
time: 903 us; the launch traced here: 892 us
  waiting for transfers between devices  243 us (27%)
  other arithmetic  238 us (26%)
  matrix products  222 us (25%)
  local copies, waits for them, and re-layouts  159 us (18%)
  between operations  17 us (2%)
  blocking collectives  9.67 us (1%)
    unnamed x6, waiting for transfers between devices  119 us
    ppermute x4, waiting for transfers between devices, tensor_others(): return lax.ppermute(part, 'tensor', [(0, 1), (1, 0)])  110 us
    dot_general x6, matrix products, head_mix(): jnp.einsum('chts,cshp->cthp', mixing, low_head, preferred_element_type=jn...  50.7 us
    unnamed x499, local copies, waits for them, and re-layouts  44.9 us
    dot_general x6, matrix products, right_product(): lax.dot_general(left, weight, (((1,), (1,)), ((), ())), preferred_element...  36.8 us
    convert_element_type x4, local copies, waits for them, and re-layouts, head_mix(): values.astype(jnp.bfloat16).reshape(chunks, CHUNK, heads, HEAD_DIM)  29.8 us
    reduce_sum x8, other arithmetic, causal_conv(): weight[KERNEL - 1 - delay][None, :] * earlier * doc_masks[delay][:, None]  29.6 us
    reduce_sum x4, other arithmetic, head_mix(): return mixed + jnp.repeat(skip_gain, HEAD_DIM)[None, :] * values  27.6 us
  transfers between devices with their start and end apart: 8, of which 4 were waited for; matrix products, arithmetic and copies ran while one was open for 44% of the time, Pallas kernels for 0%

profile of v1, /device:TPU:0, one launch (start us, length us, event | category | flops | bytes accessed | tf_op | source)
XLA Modules:
  0.0 891.8 jit_solution(17091183046651739956)
XLA Ops:
  50.3 21.8 %fusion.435 = (bf16[1024,1024]{1,0:T(8,128)(2,1)}, f32[1024,1024]{1,0:T(8,128)}, bf16[1024,1024]{1,0:T(8,128)(2,1)}, f32[1024,1024]{1,0:T(8,128)S(1)}) fusion(f32[1024]{0:T(1024)S(1)} %get-tuple-element.468, f32[1021,1024]{1,0:T(8,128)} %bitcast.722, f32[1024]{0:T(1024)S(1)} %bitcast.950, f32[1024]{0:T(1024)S(1)} %get-tuple-element.467, ...), kind=kLoop, calls=%fused_computation.717 | loop fusion | flops 33554432 | bytes 46133248 | tf_op jit(solution)/shard_map/jvp()/convert_element_type | solution.py:64
  93.9 16.3 %copy.290 = f32[8,128,1024]{2,1,0:T(8,128)} copy(f32[8,128,1024]{1,2,0:T(8,128)} %bitcast.774) | data formatting | bytes 8388608 | tf_op jit(solution)/shard_map/jvp()/reshape | solution.py:66
  154.3 14.7 %multiply_reduce_fusion.15 = (f32[1024]{0:T(1024)S(1)}, f32[1024]{0:T(1024)S(1)}, f32[1024,1024]{1,0:T(8,128)}, f32[1024]{0:T(1024)S(1)}, f32[1024]{0:T(1024)S(1...) fusion(f32[1024]{0:T(1024)S(1)} %copy-done.203, f32[1024,1024]{1,0:T(8,128)} %fusion.465, ...), kind=kOutput, calls=%fused_computation.169 | convolution fusion | flops 2172645376 | bytes 46161920 | tf_op jit(solution)/shard_map/dot_general | solution.py:200
  169.0 9.7 %psum.14 = f32[4,1024]{1,0:T(4,128)S(1)} all-reduce(f32[4,1024]{1,0:T(4,128)S(1)} %pad_maximum_fusion.9), channel_id=1, replica_groups=mesh['dp'=16,'tensor'=2] {'tensor'}, use_global_device_ids=true, to_apply=%region_6.7 | all-reduce | flops 4096 | bytes 32768 | tf_op jit(solution)/shard_map/psum | solution.py:203
  178.8 19.2 %multiply_multiply_fusion.1 = (f32[1024,1024]{1,0:T(8,128)}, bf16[1024,1024]{1,0:T(8,128)(2,1)S(1)}, f32[1024]{0:T(1024)}, bf16[1024,1024]{1,0:T(8,128)(2,1)S(1)...) fusion(f32[1024,1024]{1,0:T(8,128)} %fusion.465, ...), kind=kLoop, calls=%fused_computation.152 | loop fusion | flops 54523904 | bytes 58761216 | tf_op jit(solution)/shard_map/mul | solution.py:218
  218.2 9.1 %copy.351 = f32[1024,2048]{1,0:T(8,128)} copy(f32[1024,2048]{0,1:T(8,128)} %pad_maximum_fusion) | data formatting | bytes 16777216
  257.8 13.3 %multiply_reduce_fusion.3 = (f32[1024]{0:T(1024)}, f32[1024,1024]{1,0:T(8,128)S(1)}, f32[1024,1024]{1,0:T(8,128)}) fusion(f32[1024,1024]{1,0:T(8,128)} %get-tuple-element.53, f32[1024]{0:T(1024)} %copy-done.123, f32[1021,1024]{1,0:T(8,128)} %bitcast.725, f32[1024]{0:T(1024)} %bitcast.927, f32[1024]{0:T(1024)} %copy-done.120, f32[1022,1024]{1,0:T(8,128)} %bitcast.726, ...), kind=kLoop, calls=%fused_computation.115 | loop fusion | flops 17824768 | bytes 29372416 | tf_op jit(solution)/shard_map/transpose(jvp(jvp()))/checkpoint/reduce_sum | solution.py:93
  304.6 7.7 reshape.1881
  314.9 11.4 %multiply_reduce_fusion.11 = (f32[1024]{0:T(1024)}, f32[1024,1024]{1,0:T(8,128)S(1)}, f32[1024,1024]{1,0:T(8,128)}) fusion(f32[1021,1024]{1,0:T(8,128)} %bitcast.728, f32[1024]{0:T(1024)} %copy-done.123, f32[1024,1024]{1,0:T(8,128)} %get-tuple-element.223, f32[1024,1024]{1,0:T(8,128)} %reshape.1881, f32[8,128,1024]{2,1,0:T(8,128)} %get-tuple-element.312, ...), kind=kLoop, calls=%fused_computation.123 | loop fusion | flops 15727616 | bytes 29360128 | tf_op jit(solution)/shard_map/transpose(jvp(jvp()))/checkpoint/reduce_sum | solution.py:32
  335.6 12.3 %fusion.15 = (f32[8,16,128]{2,1,0:T(8,128)}, f32[8,16,128]{2,1,0:T(8,128)}, f32[8,16,128]{2,1,0:T(8,128)S(1)}, bf16[8,128,128]{2,1,0:T(8,128)(2,1)S(1)}) fusion(f32[8,16,128]{2,1,0:T(8,128)} %copy.296, f32[8,128,128]{2,1,0:T(8,128)} %fusion.476, f32[8,16,128]{2,1,0:T(8,128)S(1)} %fusion.291, pred[8,128,128]{2,1,0:T(8,128)(4,1)} %compare_and_fusion.1, ...), kind=kOutput, calls=%fused_computation.39 | convolution fusion | flops 297615360 | bytes 5439488 | tf_op jit(solution)/shard_map/transpose(jvp(jvp()))/checkpoint/chts,cshp->cthp/dot_general | solution.py:65
  394.7 8.4 fusion.135
  420.6 13.4 %multiply_reduce_fusion.2 = (f32[1024]{0:T(1024)}, f32[1024,1024]{1,0:T(8,128)S(1)}, f32[1024,1024]{1,0:T(8,128)}) fusion(f32[1024,1024]{1,0:T(8,128)} %get-tuple-element.69, f32[1024]{0:T(1024)S(1)} %get-tuple-element.431, f32[1021,1024]{1,0:T(8,128)} %bitcast.716, f32[1024]{0:T(1024)S(1)} %bitcast.925, f32[1024]{0:T(1024)S(1)} %get-tuple-element.432, ...), kind=kLoop, calls=%fused_computation.114 | loop fusion | flops 17824768 | bytes 29372416 | tf_op jit(solution)/shard_map/transpose(jvp(jvp()))/checkpoint/reduce_sum | solution.py:93
  463.6 7.6 reshape.1883
  478.7 11.2 %fusion.17 = (f32[8,16,128]{2,1,0:T(8,128)}, f32[8,16,128]{2,1,0:T(8,128)}, f32[8,16,128]{2,1,0:T(8,128)S(1)}, bf16[8,128,128]{2,1,0:T(8,128)(2,1)S(1)}) fusion(f32[8,16,128]{2,1,0:T(8,128)S(1)} %copy.315, f32[8,128,128]{2,1,0:T(8,128)S(1)} %copy-done.92, f32[8,16,128]{2,1,0:T(8,128)S(1)} %fusion.288, pred[8,128,128]{2,1,0:T(8,128)(4,1)S(1)} %compare_and_fusion, ...), kind=kOutput, calls=%fused_computation.41 | convolution fusion | flops 297615360 | bytes 5439488 | tf_op jit(solution)/shard_map/transpose(jvp(jvp()))/checkpoint/chts,cshp->cthp/dot_general | solution.py:65
  540.8 8.5 fusion.421
  550.8 9.2 %fusion.44 = (f32[1024]{0:T(1024)S(1)}, f32[1024]{0:T(1024)S(1)}, f32[1024,1024]{1,0:T(8,128)}) fusion(f32[1024]{0:T(1024)S(1)} %copy-done.143, bf16[2,1024,1024]{2,1,0:T(8,128)(2,1)} %param.18, f32[1024]{0:T(1024)S(1)} %copy-done.145, f32[1024,1024]{1,0:T(8,128)} %fusion.135, f32[1024,1024]{1,0:T(8,128)} %fusion.479, bf16[1024,16]{1,0:T(8,128)(2,1)} %copy.309, ...), kind=kOutput, calls=%fused_computation.75 | convolution fusion | flops 2743269376 | bytes 22102016 | tf_op jit(solution)/shard_map/dot_general | solution.py:116
  561.7 23.7 %collective-permute-done.2 = f32[1024,1024]{1,0:T(8,128)} collective-permute-done((f32[1024,1024]{1,0:T(8,128)}, f32[1024,1024]{1,0:T(8,128)}, u32[]{:S(2)}, u32[]{:S(2)}) %collective-permute-start.2) | collective-permute-done | bytes 4194336 | tf_op jit(solution)/shard_map/ppermute | solution.py:130
  588.5 14.0 %maximum_maximum_fusion = bf16[2048,1296]{1,0:T(8,128)(2,1)} fusion(bf16[1024,16]{1,0:T(8,128)(2,1)} %copy-done.86, bf16[1024,256]{1,0:T(8,128)(2,1)} %get-tuple-element.319, bf16[1024,1024]{1,0:T(8,128)(2,1)} %copy-done.52, bf16[1024,16]{1,0:T(8,128)(2,1)S(1)} %copy-done.85, bf16[1024,256]{1,0:T(8,128)(2,1)} %copy-done.73, bf16[1024,1024]{1,0:T(8,128)(2,1)S(1)} %copy-done.51), kind=kLoop, calls=%fused_computation.44 | loop fusion | flops 31850496 | bytes 10616832 | tf_op jit(solution)/shard_map/concatenate | solution.py:275
  602.5 119.3 %all-reduce.100.cloned.1.call-done = f32[470016]{0:T(1024)} async-done(((f32[470016]{0:T(1024)}), f32[470016]{0:T(1024)}) %all-reduce.100.cloned.1.call-update) | async-done | bytes 1880080
  727.3 11.6 %fusion.112 = f32[1024,1296]{1,0:T(8,128)} fusion(bf16[2048,1296]{1,0:T(8,128)(2,1)} %maximum_maximum_fusion, bf16[1024,1024]{1,0:T(8,128)(2,1)} %copy-done.48, bf16[1024,1024]{1,0:T(8,128)(2,1)S(1)} %copy-done.47), kind=kOutput, calls=%fused_computation.204 | convolution fusion | flops 5444206592 | bytes 14811136 | tf_op jit(solution)/shard_map/dot_general | solution.py:122
  745.4 86.0 %collective-permute-done.3 = f32[1024,1024]{1,0:T(8,128)} collective-permute-done((f32[1024,1024]{1,0:T(8,128)}, f32[1024,1024]{1,0:T(8,128)}, u32[]{:S(2)}, u32[]{:S(2)}) %collective-permute-start.3) | collective-permute-done | bytes 4194336 | tf_op jit(solution)/shard_map/ppermute | solution.py:130
  831.4 12.0 %fusion.36 = (f32[1024]{0:T(1024)S(1)}, f32[1024]{0:T(1024)S(1)}, bf16[1,1024,1024]{2,1,0:T(8,128)(2,1)}) fusion(f32[1024]{0:T(1024)S(1)} %copy-done.138, f32[1024,1024]{1,0:T(8,128)} %fusion.135, f32[1024,1024]{1,0:T(8,128)} %collective-permute-done.2, bf16[2,1024,1024]{2,1,0:T(8,128)(2,1)} %param.18, f32[1024,1024]{1,0:T(8,128)} %get-tuple-element.82, ...), kind=kLoop, calls=%fused_computation.67 | loop fusion | flops 13629440 | bytes 31469568 | tf_op jit(solution)/shard_map/reduce_sum | solution.py:287
  843.5 11.8 %fusion.35 = (f32[1,1024,1024]{2,1,0:T(8,128)S(1)}, f32[1,1024,1024]{2,1,0:T(8,128)}, bf16[1,1024,1024]{2,1,0:T(8,128)(2,1)}) fusion(f32[1024]{0:T(1024)S(1)} %get-tuple-element.178, f32[1024]{0:T(1024)S(1)} %copy-done.172, f32[1024]{0:T(1024)S(1)} %copy-done.145, bf16[2,1024,1024]{2,1,0:T(8,128)(2,1)} %param.34, f32[1024]{0:T(1024)S(1)} %copy-done.138, ...), kind=kLoop, calls=%fused_computation.66 | loop fusion | flops 24117248 | bytes 44068864 | tf_op jit(solution)/shard_map/stack | solution.py:308
  869.8 13.6 %all-reduce.98.cloned.1.call-done = f32[64,256]{1,0:T(8,128)} async-done(((f32[64,256]{1,0:T(8,128)}), f32[64,256]{1,0:T(8,128)}) %all-reduce.98.cloned.1.call-update) | async-done | bytes 65552 | tf_op jit(solution)/shard_map/psum | solution.py:295
  (774 shorter events, 389.0 us)
Async XLA Ops:
  7.2 132.3 %copy-start = (bf16[1024,1024]{1,0:T(8,128)(2,1)S(1)}, bf16[1024,1024]{1,0:T(8,128)(2,1)}, u32[]{:S(2)}) copy-start(bf16[1024,1024]{1,0:T(8,128)(2,1)} %param.33) | copy-start | bytes 6291460
  7.2 553.0 %reduce-scatter.7.cloned.1.call-start = ((), (), s32[]{:S(2)}) async-start(), calls=%async_computation.5 | async-start | bytes 8912896
  8.1 77.2 %copy-start.80 = (s32[1,1024]{1,0:T(1,128)}, s32[1,1024]{1,0:T(1,128)S(1)}, u32[]{:S(2)}) copy-start(s32[1,1024]{1,0:T(1,128)S(1)} %get-tuple-element.415) | copy-start | bytes 12292
  30.0 204.7 %copy-start.98 = (pred[128,128]{1,0:T(8,128)(4,1)}, pred[128,128]{1,0:T(8,128)(4,1)S(1)}, u32[]{:S(2)}) copy-start(pred[128,128]{1,0:T(8,128)(4,1)S(1)} %iota_compare_fusion.7) | copy-start | bytes 49156
  50.3 21.8 %copy-start.175 = (f32[8,16]{1,0:T(8,128)S(1)}, f32[8,16]{1,0:T(8,128)}, u32[]{:S(2)}) copy-start(f32[8,16]{1,0:T(8,128)} %copy-done.174) | copy-start | bytes 1540
  202.4 200.8 %collective-permute-start = (f32[1024,1024]{1,0:T(8,128)}, f32[1024,1024]{1,0:T(8,128)}, u32[]{:S(2)}, u32[]{:S(2)}) collective-permute-start(f32[1024,1024]{1,0:T(8,128)} %fusion.473), channel_id=1, source_target_pairs={{0,1},{1,0},{2,3},{3,2},{4,5},{5,4},{6,7},{7,6},{8,9},{9,8},{10,11... | collective-permute-start | bytes 12582920 | tf_op jit(solution)/shard_map/ppermute | solution.py:130
  227.4 494.4 %all-reduce.100.cloned.1.call-start = ((), (), s32[]{:S(2)}) async-start(), calls=%async_computation.4 | async-start | bytes 3760128
  233.5 328.2 %collective-permute-start.1 = (f32[1024,1024]{1,0:T(8,128)}, f32[1024,1024]{1,0:T(8,128)}, u32[]{:S(2)}, u32[]{:S(2)}) collective-permute-start(f32[1024,1024]{1,0:T(8,128)} %fusion.474), channel_id=1, source_target_pairs={{0,1},{1,0},{2,3},{3,2},{4,5},{5,4},{6,7},{7,6},{8,9},{9,8},{10,11... | collective-permute-start | bytes 12582920 | tf_op jit(solution)/shard_map/ppermute | solution.py:130
  406.1 91.8 %copy-start.53 = (bf16[1024,128]{1,0:T(8,128)(2,1)}, bf16[1024,128]{1,0:T(8,128)(2,1)S(1)}, u32[]{:S(2)}) copy-start(bf16[1024,128]{1,0:T(8,128)(2,1)S(1)} %get-tuple-element.329) | copy-start | bytes 786436
  419.2 74.8 %copy-start.125 = (f32[8,16]{1,0:T(8,128)}, f32[8,16]{1,0:T(8,128)S(1)}, u32[]{:S(2)}) copy-start(f32[8,16]{1,0:T(8,128)S(1)} %slice_reduce_fusion) | copy-start | bytes 1540
  420.5 69.7 %copy-start.82 = (f32[8,128,16]{1,2,0:T(8,128)}, f32[8,128,16]{1,2,0:T(8,128)S(1)}, u32[]{:S(2)}) copy-start(f32[8,128,16]{1,2,0:T(8,128)S(1)} %copy.313) | copy-start | bytes 196612
  495.0 90.4 %collective-permute-start.2 = (f32[1024,1024]{1,0:T(8,128)}, f32[1024,1024]{1,0:T(8,128)}, u32[]{:S(2)}, u32[]{:S(2)}) collective-permute-start(f32[1024,1024]{1,0:T(8,128)} %fusion.135), channel_id=1, source_target_pairs={{0,1},{1,0},{2,3},{3,2},{4,5},{5,4},{6,7},{7,6},{8,9},{9,8},{10,11... | collective-permute-start | bytes 12582920 | tf_op jit(solution)/shard_map/ppermute | solution.py:130
  560.0 28.4 %copy-start.51 = (bf16[1024,1024]{1,0:T(8,128)(2,1)S(1)}, bf16[1024,1024]{1,0:T(8,128)(2,1)}, u32[]{:S(2)}) copy-start(bf16[1024,1024]{1,0:T(8,128)(2,1)} %copy-done.50) | copy-start | bytes 6291460
  560.0 28.4 %copy-start.85 = (bf16[1024,16]{1,0:T(8,128)(2,1)S(1)}, bf16[1024,16]{1,0:T(8,128)(2,1)}, u32[]{:S(2)}) copy-start(bf16[1024,16]{1,0:T(8,128)(2,1)} %copy-done.84) | copy-start | bytes 98308
  588.4 273.7 %reduce-scatter.5.cloned.1.call-start = ((), (), s32[]{:S(2)}) async-start(), calls=%async_computation.2 | async-start | bytes 6127616 | tf_op jit(solution)/shard_map/reduce_scatter | solution.py:274
  602.5 124.9 %copy-start.47 = (bf16[1024,1024]{1,0:T(8,128)(2,1)S(1)}, bf16[1024,1024]{1,0:T(8,128)(2,1)}, u32[]{:S(2)}) copy-start(bf16[1024,1024]{1,0:T(8,128)(2,1)} %copy-done.45) | copy-start | bytes 6291460
  738.9 92.6 %copy-start.138 = (f32[1024]{0:T(1024)S(1)}, f32[1024]{0:T(1024)}, u32[]{:S(2)}) copy-start(f32[1024]{0:T(1024)} %param.20) | copy-start | bytes 12292
  738.9 144.5 %all-reduce.98.cloned.1.call-start = ((), (), s32[]{:S(2)}) async-start(), calls=%async_computation.3 | async-start | bytes 131072 | tf_op jit(solution)/shard_map/psum | solution.py:295
  739.0 92.5 %collective-permute-start.3 = (f32[1024,1024]{1,0:T(8,128)}, f32[1024,1024]{1,0:T(8,128)}, u32[]{:S(2)}, u32[]{:S(2)}) collective-permute-start(f32[1024,1024]{1,0:T(8,128)} %get-tuple-element.82), channel_id=1, source_target_pairs={{0,1},{1,0},{2,3},{3,2},{4,5},{5,4},{6,7},{7,6},{8,9},{9,8},{10,11... | collective-permute-start | bytes 12582920 | tf_op jit(solution)/shard_map/ppermute | solution.py:130
  745.4 98.0 %copy-start.9 = (bf16[2,1024,1024]{2,1,0:T(8,128)(2,1)S(1)}, bf16[2,1024,1024]{2,1,0:T(8,128)(2,1)}, u32[]{:S(2)}) copy-start(bf16[2,1024,1024]{2,1,0:T(8,128)(2,1)} %param.18) | copy-start | bytes 12582916
  745.4 98.0 %copy-start.28 = (f32[1024,1024]{1,0:T(8,128)S(1)}, f32[1024,1024]{1,0:T(8,128)}, u32[]{:S(2)}) copy-start(f32[1024,1024]{1,0:T(8,128)} %fusion.135) | copy-start | bytes 12582916
  745.4 98.0 %copy-start.29 = (f32[1024,1024]{1,0:T(8,128)S(1)}, f32[1024,1024]{1,0:T(8,128)}, u32[]{:S(2)}) copy-start(f32[1024,1024]{1,0:T(8,128)} %get-tuple-element.82) | copy-start | bytes 12582916
  745.4 98.0 %copy-start.171 = (f32[1024]{0:T(1024)S(1)}, f32[1024]{0:T(1024)}, u32[]{:S(2)}) copy-start(f32[1024]{0:T(1024)} %get-tuple-element.420) | copy-start | bytes 12292
  745.4 98.0 %copy-start.172 = (f32[1024]{0:T(1024)S(1)}, f32[1024]{0:T(1024)}, u32[]{:S(2)}) copy-start(f32[1024]{0:T(1024)} %get-tuple-element.466) | copy-start | bytes 12292
  (223 other events, 1252.3 us)
Sparse Core Ops, SparseCore 0:
  227.5 105.5 reduce-scatter.6
  588.5 133.1 all-reduce.99
  739.0 81.1 reduce-scatter.4
  863.7 19.6 all-reduce.97
